TPU v7x, 32 devices: a whole 2x2x4 slice. The times are simulated.
32 devices in a mesh: grp: 4 (over x, core), dev: 8 (over z, y).
Axes of the slice: x: 2, y: 2, z: 4, core: 2. Of those that a mesh axis runs over, the one named last changes fastest.
Arguments:
- traces: float32 [32, 16, 128], P(('grp', 'dev')), parts along dimension 0
- half_window: int32 [32], P(('grp', 'dev')), parts along dimension 0, may hold values from 4 to 23
- dip_slopes: int32 [9], replicated, may hold values from -4 to 4, as said below
Outputs:
- coherence: float32 [32, 16, 128], P('grp', 'dev'), parts along dimension 0
There are 4 independent parts, one for each index of `grp`. A program takes and returns all parts, laid end to end along the dimension named above; an argument that names none is the same for every part. Nothing has to cross between parts.
Inputs may be any that keep to these rules, and one draw needn't show every extreme that they name: `dip_slopes`: each trial dip is a whole number of samples per shot; both extreme dips occur.
All inputs are finite; a program needn't handle non-finite values.
Results may differ from a plain program's by a relative error of at most 0.00005.
Values sent between devices are 32-bit elements; how exact they have to be, the bound alone decides.
A program may use at most 64 MiB of HBM per device.

v0:
```python
import jax
import jax.numpy as jnp
from jax import lax
from jax.sharding import PartitionSpec as P

floor_level = 0.05


def extended_2(value, sides, width):
    for axis, dim in sides:
        size, length = (lax.axis_size(axis), value.shape[dim])
        up = [(i, (i + 1) % size) for i in range(size - 1)]
        down = [(j, i) for i, j in up]
        last = lax.slice_in_dim(value, length - width, length, axis=dim)
        initial = lax.slice_in_dim(value, 0, width, axis=dim)
        before = lax.ppermute(last, axis, up)
        after = lax.ppermute(initial, axis, down)
        value = jnp.concatenate([before, value, after], axis=dim)
    return value


def gain_control(traces, half_window):
    samples = jnp.arange(traces.shape[-1], dtype=jnp.int32)
    distance = jnp.abs(samples[:, None] - samples[None, :])
    window_mask = (distance[None, :, :] <= half_window[:, None, None]).astype(jnp.float32)
    window_count = jnp.sum(window_mask, axis=1)
    power_sum = jnp.einsum(
        "srt,stu->sru", traces * traces, window_mask, precision=lax.Precision.HIGHEST
    )
    mean_square = power_sum / window_count[:, None, :]
    return traces * lax.rsqrt(jnp.maximum(mean_square, floor_level))


def semblance_scan(widened, dip_slopes):
    shot_count = widened.shape[0]
    wide = widened.shape[1]
    length = widened.shape[2]
    inner = wide - 4
    padded = jnp.pad(widened, ((2, 2), (0, 0), (13, 13)))
    extended = length + 10
    later = jnp.arange(extended, dtype=jnp.int32)[:, None]
    earlier = jnp.arange(length, dtype=jnp.int32)[None, :]
    lag_gap = later - earlier
    time_band = ((lag_gap >= 0) & (lag_gap <= 10)).astype(jnp.float32)
    coherent = None
    for which in range(dip_slopes.shape[0]):
        slope = dip_slopes[which]
        stacked = jnp.zeros((shot_count, wide, extended), jnp.float32)
        energy_sum = jnp.zeros((shot_count, wide, extended), jnp.float32)
        for member in range(5):
            offset = member - 2
            rows = padded[member : member + shot_count, :, :]
            start = 8 + offset * slope
            shifted = lax.dynamic_slice_in_dim(rows, start, extended, 2)
            stacked = stacked + shifted
            energy_sum = energy_sum + shifted * shifted
        squared = stacked * stacked
        squared_rows = squared[:, 0:inner, :]
        energy_rows = energy_sum[:, 0:inner, :]
        for across in range(1, 5):
            squared_rows = squared_rows + squared[:, across : across + inner, :]
            energy_rows = energy_rows + energy_sum[:, across : across + inner, :]
        numerator = jnp.dot(
            squared_rows.reshape(shot_count * inner, extended),
            time_band,
            precision=lax.Precision.HIGHEST,
            preferred_element_type=jnp.float32,
        )
        denominator = jnp.dot(
            energy_rows.reshape(shot_count * inner, extended),
            time_band,
            precision=lax.Precision.HIGHEST,
            preferred_element_type=jnp.float32,
        )
        current = (numerator / (5.0 * denominator + 1.0)).reshape(shot_count, inner, length)
        coherent = current if coherent is None else jnp.maximum(coherent, current)
    return coherent


def body(traces, half_window, dip_slopes):
    balanced = gain_control(traces, half_window)
    gathered = lax.all_to_all(balanced, "dev", split_axis=1, concat_axis=0, tiled=True)
    widened = extended_2(gathered, (("dev", 1),), 2)
    return semblance_scan(widened, dip_slopes)


def solution(mesh):
    return jax.shard_map(
        body,
        mesh=mesh,
        in_specs=(P(("grp", "dev"), None, None), P(("grp", "dev")), P()),
        out_specs=P("grp", "dev", None),
        check_vma=False,
    )
```

profile of v0, /device:TPU:0, one launch (start us, length us, event | category | flops | bytes accessed | tf_op | source)
XLA Modules:
  0.0 51.2 jit_solution(14853539897846402921)
XLA Ops:
  0.7 1.5 %fusion.29 = f32[1,16,128]{2,1,0:T(8,128)} fusion(f32[1,16,128]{2,1,0:T(8,128)} %param.3, s32[]{:T(128)} %bitcast.104, f32[128]{0:T(128)S(1)} %convert_reduce_fusion), kind=kOutput, calls=%fused_computation.39 | convolution fusion | flops 3203072 | bytes 16900 | tf_op jit(solution)/shard_map/srt,stu->sru/dot_general | solution.py:27
  2.2 7.4 %all-to-all-start = ((f32[1,16,128]{2,0,1:T(1,128)}), f32[1,16,128]{2,0,1:T(1,128)S(1)}, u32[]{:S(2)}, u32[]{:S(2)}) async-start(f32[1,16,128]{2,0,1:T(1,128)} %bitcast.4), calls=%async_computation | async-start | bytes 16384 | tf_op jit(solution)/shard_map/all_to_all | solution.py:82
  9.7 0.7 %fusion.105 = (s32[1]{0:T(128)}, s32[1]{0:T(128)}, s32[1]{0:T(128)}, s32[1]{0:T(128)}, s32[1]{0:T(128)}, /*index=5*/s32[1]{0:T(128)}, s32[1]{0:T(128)}, s32[1]{0:T(128)}, s32[1]{0:T(128)}) fusion(s32[9]{0:T(128)S(1)} %copy-done), kind=kLoop, calls=%fused_computation.196 | loop fusion | bytes 72 | tf_op jit(solution)/shard_map/slice | solution.py:47
  32.6 1.3 %collective-permute-start.1 = (f32[8,2,128]{2,1,0:T(2,128)S(1)}, f32[8,2,128]{2,1,0:T(2,128)S(1)}, u32[]{:S(2)}, u32[]{:S(2)}) collective-permute-start(f32[8,2,128]{2,1,0:T(2,128)S(1)} %bitcast.106), channel_id=1, source_target_pairs={{1,0},{2,1},{3,2},{4,3},{5,4},{6,5},{7,6},{9,8},{10,9},{11,10},{12... | collective-permute-start | bytes 24584 | tf_op jit(solution)/shard_map/ppermute | solution.py:17
  33.9 4.5 %collective-permute-start = (f32[8,2,128]{2,1,0:T(2,128)S(1)}, f32[8,2,128]{2,1,0:T(2,128)S(1)}, u32[]{:S(2)}, u32[]{:S(2)}) collective-permute-start(f32[8,2,128]{2,1,0:T(2,128)S(1)} %bitcast.107), channel_id=1, source_target_pairs={{0,1},{1,2},{2,3},{3,4},{4,5},{5,6},{6,7},{8,9},{9,10},{10,11},{11... | collective-permute-start | bytes 24584 | tf_op jit(solution)/shard_map/ppermute | solution.py:16
  44.7 0.3 add_multiply_fusion.6
  45.2 0.3 multiply_add_fusion
  46.0 0.1 fusion.57
  46.1 0.3 add_multiply_fusion
  46.5 0.3 add_multiply_fusion.3
  46.9 0.1 fusion.54
  47.3 0.1 fusion.51
  47.4 0.3 multiply_add_fusion.1
  48.1 0.2 add_multiply_fusion.1
  48.6 0.1 fusion.42
  49.0 0.1 fusion.25
  49.2 0.2 fusion.23
  49.4 0.2 fusion.20
  49.5 0.2 fusion.17
  49.7 0.2 fusion.14
  49.9 0.2 fusion.11
  50.1 0.2 fusion.8
  50.2 0.2 fusion.5
  50.4 0.8 %fusion.2 = f32[16,128]{1,0:T(8,128)} fusion(f32[16,128]{1,0:T(8,128)S(1)} %fusion.5, f32[16,128]{1,0:T(8,128)S(1)} %fusion.39, f32[16,138]{1,0:T(8,128)S(1)} %reshape.379), kind=kOutput, calls=%fused_computation.3 | convolution fusion | flops 3470336 | bytes 33408 | tf_op jit(solution)/shard_map/dot_general | solution.py:69
  (43 shorter events, 1.8 us)
Async XLA Ops:
  2.2 7.4 %copy-start = (s32[9]{0:T(128)S(1)}, s32[9]{0:T(128)}, u32[]{:S(2)}) copy-start(s32[9]{0:T(128)} %param.5) | copy-start | bytes 112
  2.2 30.3 %all-to-all-start = ((f32[1,16,128]{2,0,1:T(1,128)}), f32[1,16,128]{2,0,1:T(1,128)S(1)}, u32[]{:S(2)}, u32[]{:S(2)}) async-start(f32[1,16,128]{2,0,1:T(1,128)} %bitcast.4), calls=%async_computation | async-start | bytes 16384 | tf_op jit(solution)/shard_map/all_to_all | solution.py:82
  32.6 12.0 %collective-permute-start.1 = (f32[8,2,128]{2,1,0:T(2,128)S(1)}, f32[8,2,128]{2,1,0:T(2,128)S(1)}, u32[]{:S(2)}, u32[]{:S(2)}) collective-permute-start(f32[8,2,128]{2,1,0:T(2,128)S(1)} %bitcast.106), channel_id=1, source_target_pairs={{1,0},{2,1},{3,2},{4,3},{5,4},{6,5},{7,6},{9,8},{10,9},{11,10},{12... | collective-permute-start | bytes 24584 | tf_op jit(solution)/shard_map/ppermute | solution.py:17
  33.9 10.7 %collective-permute-start = (f32[8,2,128]{2,1,0:T(2,128)S(1)}, f32[8,2,128]{2,1,0:T(2,128)S(1)}, u32[]{:S(2)}, u32[]{:S(2)}) collective-permute-start(f32[8,2,128]{2,1,0:T(2,128)S(1)} %bitcast.107), channel_id=1, source_target_pairs={{0,1},{1,2},{2,3},{3,4},{4,5},{5,6},{6,7},{8,9},{9,10},{10,11},{11... | collective-permute-start | bytes 24584 | tf_op jit(solution)/shard_map/ppermute | solution.py:16
where the time goes:
time: 51.9 us; the launch traced here: 51.2 us
  between operations  29.4 us (57%)
  starting transfers between devices  13.3 us (26%)
  matrix products  4.8 us (9%)
  other arithmetic  2.68 us (5%)
  local copies, waits for them, and re-layouts  1.05 us (2%)
    all_to_all x1, starting transfers between devices, body(): lax.all_to_all(balanced, 'dev', split_axis=1, concat_axis=0, tiled=True)  7.41 us
    ppermute x1, starting transfers between devices, extended_2(): before = lax.ppermute(last, axis, up)  4.55 us
    dot_general x9, matrix products, semblance_scan(): jnp.dot(energy_rows.reshape(shot_count * inner, extended), time_band, pre...  2.05 us
    dot_general x1, matrix products, gain_control(): jnp.einsum('srt,stu->sru', traces * traces, window_mask, precision=lax.Pr...  1.54 us
    ppermute x1, starting transfers between devices, extended_2(): after = lax.ppermute(initial, axis, down)  1.29 us
    mul x4, other arithmetic, semblance_scan(): squared = stacked * stacked  1.22 us
    dot_general x9, matrix products, semblance_scan(): jnp.dot(squared_rows.reshape(shot_count * inner, extended), time_band, pr...  1.21 us
  transfers between devices with their start and end apart: 3, of which 0 were waited for; matrix products, arithmetic and copies ran while one was open for 1% of the time, Pallas kernels for 0%

commit v1 on v0

v1 whole, which is shorter than its diff:
```python
import functools

import jax
import jax.numpy as jnp
from jax import lax
from jax.experimental import pallas as pl
from jax.experimental.pallas import tpu as pltpu
from jax.sharding import PartitionSpec as P

MESH = pl.DeviceIdType.MESH
FLOOR = 0.05
HALF_RECV = 2
HALF_TIME = 5
MAXDIP = 4
TILE = 8


def ahead(value, amount):
    length = value.shape[-1]
    shift = (-amount) % length
    return value if shift == 0 else pltpu.roll(value, shift, value.ndim - 1)


def box(value):
    two = value + ahead(value, 1)
    four = two + ahead(two, 2)
    eight = four + ahead(four, 4)
    return (eight + ahead(two, 8)) + ahead(value, 10)


def recv_sums(rows, inner):
    if inner == 2:
        common = (rows[1] + rows[2]) + (rows[3] + rows[4])
        return [common + rows[0], common + rows[5]]
    return [functools.reduce(jnp.add, rows[o : o + 5]) for o in range(inner)]


def kernel(
    n, shots, recv, inner, rp,
    traces_ref, window_ref, dips_ref, out_ref,
    pad, send, buf, boxed, send_sem, recv_sem,
):
    length = traces_ref.shape[-1]
    me = lax.axis_index("dev")
    unroll = n <= 16

    def each(low, high, body):
        if unroll:
            for i in range(low, high):
                body(i)
        else:
            lax.fori_loop(low, high, lambda i, c: (body(i), c)[1], 0)

    barrier = pltpu.get_barrier_semaphore()

    def greet(d):
        pl.semaphore_signal(
            barrier, inc=1, device_id={"dev": lax.rem(me + d, n)}, device_id_type=MESH
        )

    each(1, n, greet)

    half = window_ref[0]
    values = traces_ref[0]
    later = lax.broadcasted_iota(jnp.int32, (length, length), 0)
    earlier = lax.broadcasted_iota(jnp.int32, (length, length), 1)
    near = (jnp.abs(later - earlier) <= half).astype(jnp.float32)
    power = jnp.dot(
        values * values, near,
        precision=lax.Precision.HIGHEST, preferred_element_type=jnp.float32,
    )
    sample = lax.broadcasted_iota(jnp.int32, (1, length), 1)
    count = jnp.minimum(sample + half, length - 1) - jnp.maximum(sample - half, 0) + 1
    balanced = values * lax.rsqrt(jnp.maximum(power / count.astype(jnp.float32), FLOOR))
    pad[0:HALF_RECV, :] = jnp.zeros((HALF_RECV, length), jnp.float32)
    pad[HALF_RECV : HALF_RECV + recv, :] = balanced
    tail = pad.shape[0] - HALF_RECV - recv
    pad[HALF_RECV + recv :, :] = jnp.zeros((tail, length), jnp.float32)

    def pack(d):
        send[d] = pad[pl.ds(d * inner, rp), :]

    each(0, n, pack)
    edge = jnp.zeros((2 * rp, length), jnp.float32)
    buf[0 : 2 * rp, :] = edge
    buf[(shots + 2) * rp :, :] = edge
    for ref in range(2 * inner):
        boxed[ref, 0:TILE, :] = jnp.zeros((TILE, length), jnp.float32)
        boxed[ref, TILE + shots :, :] = jnp.zeros((TILE, length), jnp.float32)
    weights = []
    for dip in range(-MAXDIP, MAXDIP + 1):
        found = dips_ref[0] == dip
        for i in range(1, dips_ref.shape[0]):
            found = jnp.logical_or(found, dips_ref[i] == dip)
        weights.append(jnp.where(found, 1.0, 0.0).astype(jnp.float32))

    pl.semaphore_wait(barrier, n - 1)

    def block(shot):
        return buf.at[pl.ds(pl.multiple_of((shot + 2) * rp, TILE), rp), :]

    def outgoing(d):
        peer = lax.rem(me + d, n)
        return pltpu.make_async_remote_copy(
            src_ref=send.at[peer],
            dst_ref=block(me),
            send_sem=send_sem.at[d],
            recv_sem=recv_sem.at[d],
            device_id={"dev": peer},
            device_id_type=MESH,
        )

    each(1, n, lambda d: outgoing(d).start())
    buf[pl.ds(pl.multiple_of((me + 2) * rp, TILE), rp), :] = send[me]

    def arrived(d):
        source = lax.rem(me + n - d, n)
        pltpu.make_async_remote_copy(
            src_ref=send.at[source],
            dst_ref=block(source),
            send_sem=send_sem.at[d],
            recv_sem=recv_sem.at[d],
            device_id={"dev": source},
            device_id_type=MESH,
        ).wait_recv()

    each(1, n, arrived)

    lane = lax.broadcasted_iota(jnp.int32, (TILE, length), 1)
    sides = (lane < 3 * length // 4, lane >= length // 4)

    def member(first, r, k):
        start = (first + k + 2) * rp + r
        return buf[pl.ds(start, TILE, stride=rp), :]

    def energies(first):
        squares = []
        for r in range(inner + 4):
            own = member(first, r, 0)
            squares.append(own * own)
        for o, total in enumerate(recv_sums(squares, inner)):
            for side in range(2):
                boxed[2 * o + side, pl.ds(first + TILE, TILE), :] = box(
                    jnp.where(sides[side], total, 0.0)
                )

    def scan(first):
        best = [[None, None] for _ in range(inner)]
        for dip in range(-MAXDIP, MAXDIP + 1):
            for side in range(2):
                squares = []
                for r in range(inner + 4):
                    terms = [
                        ahead(jnp.where(sides[side], member(first, r, k), 0.0), k * dip)
                        for k in range(-2, 3)
                    ]
                    total = ((terms[0] + terms[1]) + (terms[3] + terms[4])) + terms[2]
                    squares.append(total * total)
                for o, total in enumerate(recv_sums(squares, inner)):
                    terms = [
                        ahead(boxed[2 * o + side, pl.ds(first + TILE + k, TILE), :], k * dip)
                        for k in range(-2, 3)
                    ]
                    energy = ((terms[0] + terms[1]) + (terms[3] + terms[4])) + terms[2]
                    current = box(total) * weights[dip + MAXDIP] / (5.0 * energy + 1.0)
                    held = best[o][side]
                    best[o][side] = current if held is None else jnp.maximum(held, current)
        for o in range(inner):
            low, high = (ahead(best[o][side], -HALF_TIME) for side in range(2))
            out_ref[o, pl.ds(first, TILE), :] = jnp.where(lane < length // 2, low, high)

    blocks = shots // TILE
    if blocks == 1:
        energies(0)
        scan(0)
    else:
        lax.fori_loop(0, blocks, lambda i, c: (energies(pl.multiple_of(i * TILE, TILE)), c)[1], 0)
        lax.fori_loop(0, blocks, lambda i, c: (scan(pl.multiple_of(i * TILE, TILE)), c)[1], 0)

    each(1, n, lambda d: outgoing(d).wait_send())


def body(n, traces, half_window, dip_slopes):
    _, recv, length = traces.shape
    shots = n
    inner = recv // n
    rp = -(-(inner + 2 * HALF_RECV) // TILE) * TILE
    result = pl.pallas_call(
        functools.partial(kernel, n, shots, recv, inner, rp),
        out_shape=jax.ShapeDtypeStruct((inner, shots, length), jnp.float32),
        in_specs=[
            pl.BlockSpec(memory_space=pltpu.VMEM),
            pl.BlockSpec(memory_space=pltpu.SMEM),
            pl.BlockSpec(memory_space=pltpu.SMEM),
        ],
        out_specs=pl.BlockSpec(memory_space=pltpu.VMEM),
        scratch_shapes=[
            pltpu.VMEM((recv + rp, length), jnp.float32),
            pltpu.VMEM((n, rp, length), jnp.float32),
            pltpu.VMEM(((shots + 4) * rp, length), jnp.float32),
            pltpu.VMEM((2 * inner, shots + 2 * TILE, length), jnp.float32),
            pltpu.SemaphoreType.DMA((n,)),
            pltpu.SemaphoreType.DMA((n,)),
        ],
        compiler_params=pltpu.CompilerParams(
            collective_id=0, has_side_effects=True, vmem_limit_bytes=24 * 1024 * 1024
        ),
    )(traces, half_window, dip_slopes)
    return jnp.swapaxes(result, 0, 1)


def solution(mesh):
    return jax.shard_map(
        functools.partial(body, mesh.shape["dev"]),
        mesh=mesh,
        in_specs=(P(("grp", "dev"), None, None), P(("grp", "dev")), P()),
        out_specs=P("grp", "dev", None),
        check_vma=False,
    )
```

time: 51.9 us -> 14.9 us (0.29)
  between operations: 29.4 us -> 0.69 us
  starting transfers between devices: 13.3 us -> 0 us
  Pallas kernels: 0 us -> 12.7 us
  matrix products: 4.8 us -> 0 us
  other arithmetic: 2.68 us -> 0 us
    pallas_call x0 -> x1, Pallas kernels: none -> 12.7 us  [body(): pl.pallas_call(functools.partial(kernel, n, shots, recv, inner, rp), out_...]
    all_to_all x1 -> x0, starting transfers between devices: 7.41 us -> none  [body(): lax.all_to_all(balanced, 'dev', split_axis=1, concat_axis=0, tiled=True)]
    ppermute x2 -> x0, starting transfers between devices: 5.84 us -> none  [the longest x1 4.55 us: extended_2(): before = lax.ppermute(last, axis, up)]
    dot_general x19 -> x0, matrix products: 4.8 us -> none  [the longest x9 2.05 us: semblance_scan(): jnp.dot(energy_rows.reshape(shot_count * inner, extended), time_band, pre...]
    add x14 -> x0, other arithmetic: 1.31 us -> none  [the longest x2 0.68 us: semblance_scan(): energy_sum = energy_sum + shifted * shifted]
    mul x4 -> x0, other arithmetic: 1.22 us -> none  [semblance_scan(): squared = stacked * stacked]
    slice x2 -> x0, local copies, waits for them, and re-layouts: 0.72 us -> none  [the longest x1 0.7 us: semblance_scan(): slope = dip_slopes[which]]
    unnamed x2 -> x4, local copies, waits for them, and re-layouts: 0.01 us -> 0.69 us
  transfers between devices with their start and end apart: 3 -> 0, of which waited for: 0 -> 0; matrix products, arithmetic and copies ran while one was open for 1% -> 0% of each run, Pallas kernels for 0% -> 0%
where the time goes in v1:
time: 14.9 us; the launch traced here: 14.7 us
  Pallas kernels  12.7 us (85%)
  local copies, waits for them, and re-layouts  1.3 us (9%)
  between operations  0.69 us (5%)
    pallas_call x1, Pallas kernels, body(): pl.pallas_call(functools.partial(kernel, n, shots, recv, inner, rp), out_...  12.7 us
    unnamed x4, local copies, waits for them, and re-layouts  0.69 us
    transpose x1, local copies, waits for them, and re-layouts, body(): return jnp.swapaxes(result, 0, 1)  0.6 us

profile of v1, /device:TPU:0, one launch (start us, length us, event | category | flops | bytes accessed | tf_op | source)
XLA Modules:
  0.0 14.7 jit_solution(6966406330225961213)
XLA Ops:
  0.0 0.0 copy-start.1
  0.7 0.0 copy-done.1
  0.7 0.0 copy-start
  0.7 0.7 %copy-done = f32[1,16,128]{2,1,0:T(8,128)S(1)} copy-done((f32[1,16,128]{2,1,0:T(8,128)S(1)}, f32[1,16,128]{2,1,0:T(8,128)}, u32[]{:S(2)}) %copy-start) | copy-done | bytes 8216
  1.4 12.7 %shard_map.37 = f32[2,8,128]{2,1,0:T(8,128)S(1)} custom-call(f32[1,16,128]{2,1,0:T(8,128)S(1)} %copy-done, s32[1]{0:T(128)S(6)} %copy.5.window_ref, s32[9]{0:T(128)S(1)} %copy-done.1), custom_call_target="tpu_custom_call" | custom-call | tf_op jit(solution)/shard_map/pallas_call | solution.py:188
  14.1 0.6 %copy.4 = f32[8,2,128]{2,1,0:T(2,128)} copy(f32[8,2,128]{2,0,1:T(8,128)S(1)} %bitcast.1) | data formatting | bytes 16384 | tf_op jit(solution)/shard_map/transpose | solution.py:209
Async XLA Ops:
  0.0 0.7 %copy-start.1 = (s32[9]{0:T(128)S(1)}, s32[9]{0:T(128)}, u32[]{:S(2)}) copy-start(s32[9]{0:T(128)} %dips_ref.1) | copy-start | bytes 112
  0.7 0.7 %copy-start = (f32[1,16,128]{2,1,0:T(8,128)S(1)}, f32[1,16,128]{2,1,0:T(8,128)}, u32[]{:S(2)}) copy-start(f32[1,16,128]{2,1,0:T(8,128)} %traces_ref.1) | copy-start | bytes 24580

commit v2 on v1

v2 whole, which is shorter than its diff:
```python
import functools

import jax
import jax.numpy as jnp
from jax import lax
from jax.experimental import pallas as pl
from jax.experimental.pallas import tpu as pltpu
from jax.sharding import PartitionSpec as P

MESH = pl.DeviceIdType.MESH
FLOOR = 0.05
HALF_RECV = 2
HALF_TIME = 5
MAXDIP = 4
TILE = 8


def ahead(value, amount):
    length = value.shape[-1]
    shift = (length - amount) % length if isinstance(amount, int) else lax.rem(length - amount, length)
    return value if isinstance(amount, int) and amount == 0 else pltpu.roll(value, shift, value.ndim - 1)


def centred_box(value):
    three = (ahead(value, -1) + ahead(value, 1)) + value
    nine = (ahead(three, -3) + ahead(three, 3)) + three
    return nine + (ahead(value, -5) + ahead(value, 5))


def recv_sums(rows, inner):
    if inner == 2:
        common = (rows[1] + rows[2]) + (rows[3] + rows[4])
        return [common + rows[0], common + rows[5]]
    return [functools.reduce(jnp.add, rows[o : o + 5]) for o in range(inner)]


def kernel(
    n, shots, recv, inner, rp,
    traces_hbm, window_hbm, dips_hbm, out_ref,
    traces_ref, window_ref, dips_ref, load_sem,    pad, send, buf, line, summed, band, weight, send_sem, recv_sem,
):
    length = traces_hbm.shape[-1]
    me = lax.axis_index("dev")
    unroll = n <= 16
    wide = inner + 4
    shifts = sorted({k * dip for k in range(3) for dip in range(-MAXDIP, MAXDIP + 1)})

    def each(low, high, body):
        if unroll:
            for i in range(low, high):
                body(i)
        else:
            lax.fori_loop(low, high, lambda i, c: (body(i), c)[1], 0)

    barrier = pltpu.get_barrier_semaphore()

    def greet(d):
        pl.semaphore_signal(
            barrier, inc=1, device_id={"dev": lax.rem(me + d, n)}, device_id_type=MESH
        )

    each(1, n, greet)

    loads = [
        pltpu.make_async_copy(src, dst, load_sem.at[i])
        for i, (src, dst) in enumerate(
            ((window_hbm, window_ref), (traces_hbm, traces_ref), (dips_hbm, dips_ref))
        )
    ]
    for load in loads:
        load.start()
    edge = jnp.zeros((2 * rp, length), jnp.float32)
    buf[0 : 2 * rp, :] = edge
    buf[(shots + 2) * rp :, :] = edge
    blank = jnp.zeros((TILE, length), jnp.float32)
    for which in range(len(shifts)):
        for row in range(2 * wide + inner):
            line[which, row, 0:TILE, :] = blank
            line[which, row, TILE + shots :, :] = blank
    for load in loads:
        load.wait()

    half = window_ref[0]
    values = traces_ref[0]
    later = lax.broadcasted_iota(jnp.int32, (length, length), 0)
    earlier = lax.broadcasted_iota(jnp.int32, (length, length), 1)
    near = (jnp.abs(later - earlier) <= half).astype(jnp.float32)
    power = jnp.dot(
        values * values, near,
        precision=lax.Precision.HIGHEST, preferred_element_type=jnp.float32,
    )
    sample = lax.broadcasted_iota(jnp.int32, (1, length), 1)
    count = jnp.minimum(sample + half, length - 1) - jnp.maximum(sample - half, 0) + 1
    balanced = values * lax.rsqrt(jnp.maximum(power / count.astype(jnp.float32), FLOOR))
    pad[0:HALF_RECV, :] = jnp.zeros((HALF_RECV, length), jnp.float32)
    pad[HALF_RECV : HALF_RECV + recv, :] = balanced
    tail = pad.shape[0] - HALF_RECV - recv
    pad[HALF_RECV + recv :, :] = jnp.zeros((tail, length), jnp.float32)

    def pack(d):
        send[d] = pad[pl.ds(d * inner, rp), :]

    each(0, n, pack)
    pl.semaphore_wait(barrier, n - 1)

    def block(shot):
        return buf.at[pl.ds(pl.multiple_of((shot + 2) * rp, TILE), rp), :]

    def outgoing(d):
        peer = lax.rem(me + d, n)
        return pltpu.make_async_remote_copy(
            src_ref=send.at[peer],
            dst_ref=block(me),
            send_sem=send_sem.at[d],
            recv_sem=recv_sem.at[d],
            device_id={"dev": peer},
            device_id_type=MESH,
        )

    each(1, n, lambda d: outgoing(d).start())
    for dip in range(-MAXDIP, MAXDIP + 1):
        found = dips_ref[0] == dip
        for i in range(1, dips_ref.shape[0]):
            found = jnp.logical_or(found, dips_ref[i] == dip)
        weight[dip + MAXDIP] = jnp.where(found, 1.0, 0.0).astype(jnp.float32)

    source = lax.broadcasted_iota(jnp.int32, (2 * length, length), 0)
    output = lax.broadcasted_iota(jnp.int32, (2 * length, length), 1)
    in_low = source < length
    at = jnp.where(in_low, source, source - length)
    at = jnp.where(in_low & (at >= 3 * length // 4), at - length, at)
    at = jnp.where(~in_low & (at < length // 4), at + length, at)
    adds = (jnp.abs(at - output) <= HALF_TIME) & (in_low == (output < length // 2))
    band[...] = adds.astype(jnp.float32).astype(jnp.bfloat16)
    buf[pl.ds(pl.multiple_of((me + 2) * rp, TILE), rp), :] = send[me]

    def arrived(d):
        source = lax.rem(me + n - d, n)
        pltpu.make_async_remote_copy(
            src_ref=send.at[source],
            dst_ref=block(source),
            send_sem=send_sem.at[d],
            recv_sem=recv_sem.at[d],
            device_id={"dev": source},
            device_id_type=MESH,
        ).wait_recv()

    each(1, n, arrived)

    lane = lax.broadcasted_iota(jnp.int32, (TILE, length), 1)
    early, late = lane < 3 * length // 4, lane >= length // 4

    def masks(amount):
        if amount > 0:
            wrapped = lane >= length - amount
            return early | wrapped, late & ~wrapped
        wrapped = lane < -amount
        return early & ~wrapped, late | wrapped

    def spread(first):
        here = pl.ds(first + TILE, TILE)
        owns = [buf[pl.ds((first + 2) * rp + r, TILE, stride=rp), :] for r in range(wide)]
        boxes = []
        for total in recv_sums([own * own for own in owns], inner):
            boxes.append(
                [centred_box(jnp.where(keep, total, 0.0)) for keep in (early, late)]
            )
        for which, amount in enumerate(shifts):
            low, high = masks(amount)
            for r, own in enumerate(owns):
                moved = ahead(own, amount)
                line[which, 2 * r, here, :] = jnp.where(low, moved, 0.0)
                line[which, 2 * r + 1, here, :] = jnp.where(high, moved, 0.0)
            target = lane - amount
            target = jnp.where(target < 0, target + length, target)
            target = jnp.where(target >= length, target - length, target)
            for o, (before, after) in enumerate(boxes):
                line[which, 2 * wide + o, here, :] = ahead(
                    jnp.where(target < length // 2, before, after), amount
                )

    def dip_sum(first, row, dip):
        terms = [
            line[shifts.index(k * dip), row, pl.ds(first + TILE + k, TILE), :]
            for k in range(-2, 3)
        ]
        return ((terms[0] + terms[1]) + (terms[3] + terms[4])) + terms[2]

    def scan(first):
        dips = range(-MAXDIP, MAXDIP + 1)
        for i, dip in enumerate(dips):
            for side in range(2):
                squares = []
                for r in range(wide):
                    total = dip_sum(first, 2 * r + side, dip)
                    squares.append(total * total)
                for o, total in enumerate(recv_sums(squares, inner)):
                    row = (i * inner + o) * TILE
                    summed[row : row + TILE, side * length : (side + 1) * length] = total
        value = summed[...]
        numerator = None
        for _ in range(3):
            piece = value.astype(jnp.bfloat16)
            value = value - piece.astype(jnp.float32)
            term = jnp.dot(piece, band[...], preferred_element_type=jnp.float32)
            numerator = term if numerator is None else numerator + term
        for o in range(inner):
            best = None
            for i, dip in enumerate(dips):
                row = (i * inner + o) * TILE
                energy = dip_sum(first, 2 * wide + o, dip)
                current = numerator[row : row + TILE] * weight[i] / (5.0 * energy + 1.0)
                best = current if best is None else jnp.maximum(best, current)
            out_ref[o, pl.ds(first, TILE), :] = best

    energies = spread

    blocks = shots // TILE
    if blocks == 1:
        energies(0)
        scan(0)
    else:
        lax.fori_loop(0, blocks, lambda i, c: (energies(pl.multiple_of(i * TILE, TILE)), c)[1], 0)
        lax.fori_loop(0, blocks, lambda i, c: (scan(pl.multiple_of(i * TILE, TILE)), c)[1], 0)

    each(1, n, lambda d: outgoing(d).wait_send())


def body(n, traces, half_window, dip_slopes):
    _, recv, length = traces.shape
    shots = n
    inner = recv // n
    rp = -(-(inner + 2 * HALF_RECV) // TILE) * TILE
    result = pl.pallas_call(
        functools.partial(kernel, n, shots, recv, inner, rp),
        out_shape=jax.ShapeDtypeStruct((inner, shots, length), jnp.float32),
        in_specs=[
            pl.BlockSpec(memory_space=pltpu.HBM),
            pl.BlockSpec(memory_space=pltpu.HBM),
            pl.BlockSpec(memory_space=pltpu.HBM),
        ],
        out_specs=pl.BlockSpec(memory_space=pltpu.VMEM),
        scratch_shapes=[
            pltpu.VMEM(traces.shape, jnp.float32),
            pltpu.SMEM(half_window.shape, jnp.int32),
            pltpu.SMEM(dip_slopes.shape, jnp.int32),
            pltpu.SemaphoreType.DMA((3,)),
            pltpu.VMEM((recv + rp, length), jnp.float32),
            pltpu.VMEM((n, rp, length), jnp.float32),
            pltpu.VMEM(((shots + 4) * rp, length), jnp.float32),
            pltpu.VMEM((13, 3 * inner + 8, shots + 2 * TILE, length), jnp.float32),
            pltpu.VMEM(((2 * MAXDIP + 1) * inner * TILE, 2 * length), jnp.float32),
            pltpu.VMEM((2 * length, length), jnp.bfloat16),
            pltpu.SMEM((2 * MAXDIP + 1,), jnp.float32),
            pltpu.SemaphoreType.DMA((n,)),
            pltpu.SemaphoreType.DMA((n,)),
        ],
        compiler_params=pltpu.CompilerParams(
            collective_id=0, has_side_effects=True, vmem_limit_bytes=32 * 1024 * 1024
        ),
    )(pltpu.with_memory_space_constraint(traces, pltpu.HBM), half_window, pltpu.with_memory_space_constraint(dip_slopes, pltpu.HBM))
    return jnp.swapaxes(result, 0, 1)


def solution(mesh):
    return jax.shard_map(
        functools.partial(body, mesh.shape["dev"]),
        mesh=mesh,
        in_specs=(P(("grp", "dev"), None, None), P(("grp", "dev")), P()),
        out_specs=P("grp", "dev", None),
        check_vma=False,
    )
```

time: 14.9 us -> 10.8 us (0.72)
  Pallas kernels: 12.7 us -> 9.35 us
  local copies, waits for them, and re-layouts: 1.3 us -> 0.6 us
    pallas_call x1, Pallas kernels: 12.7 us -> 9.35 us  [body(): pl.pallas_call(functools.partial(kernel, n, shots, recv, inner, rp), out_...]
    unnamed x4 -> x0, local copies, waits for them, and re-layouts: 0.69 us -> none
where the time goes in v2:
time: 10.8 us; the launch traced here: 10.6 us
  Pallas kernels  9.35 us (87%)
  between operations  0.66 us (6%)
  local copies, waits for them, and re-layouts  0.6 us (6%)
    pallas_call x1, Pallas kernels, body(): pl.pallas_call(functools.partial(kernel, n, shots, recv, inner, rp), out_...  9.35 us
    transpose x1, local copies, waits for them, and re-layouts, body(): return jnp.swapaxes(result, 0, 1)  0.6 us

profile of v2, /device:TPU:0, one launch (start us, length us, event | category | flops | bytes accessed | tf_op | source)
XLA Modules:
  0.0 10.6 jit_solution(2140685389938928869)
XLA Ops:
  0.7 9.4 %shard_map.37 = f32[2,8,128]{2,1,0:T(8,128)S(1)} custom-call(f32[1,16,128]{2,1,0:T(8,128)} %traces_hbm.1, s32[1]{0:T(128)S(6)} %copy.5.window_hbm, s32[9]{0:T(128)} %dips_hbm.1), custom_call_target="tpu_custom_call" | custom-call | tf_op jit(solution)/shard_map/pallas_call | solution.py:234
  10.0 0.6 %copy.4 = f32[8,2,128]{2,1,0:T(2,128)} copy(f32[8,2,128]{2,0,1:T(8,128)S(1)} %bitcast.1) | data formatting | bytes 16384 | tf_op jit(solution)/shard_map/transpose | solution.py:262

commit v3 on v2

--- a/solution.py
+++ b/solution.py
@@ -36,8 +36,8 @@
 
 def kernel(
     n, shots, recv, inner, rp,
-    traces_hbm, window_hbm, dips_hbm, out_ref,
-    traces_ref, window_ref, dips_ref, load_sem,    pad, send, buf, line, summed, band, weight, send_sem, recv_sem,
+    traces_hbm, window_ref, dips_hbm, out_ref,
+    traces_ref, dips_ref, load_sem,    pad, send, buf, line, summed, band, weight, send_sem, recv_sem,
 ):
     length = traces_hbm.shape[-1]
     me = lax.axis_index("dev")
@@ -52,6 +52,10 @@
         else:
             lax.fori_loop(low, high, lambda i, c: (body(i), c)[1], 0)
 
+    load = pltpu.make_async_copy(traces_hbm, traces_ref, load_sem.at[0])
+    load.start()
+    load_dips = pltpu.make_async_copy(dips_hbm, dips_ref, load_sem.at[1])
+    load_dips.start()
     barrier = pltpu.get_barrier_semaphore()
 
     def greet(d):
@@ -61,41 +65,23 @@
 
     each(1, n, greet)
 
-    loads = [
-        pltpu.make_async_copy(src, dst, load_sem.at[i])
-        for i, (src, dst) in enumerate(
-            ((window_hbm, window_ref), (traces_hbm, traces_ref), (dips_hbm, dips_ref))
-        )
-    ]
-    for load in loads:
-        load.start()
-    edge = jnp.zeros((2 * rp, length), jnp.float32)
-    buf[0 : 2 * rp, :] = edge
-    buf[(shots + 2) * rp :, :] = edge
-    blank = jnp.zeros((TILE, length), jnp.float32)
-    for which in range(len(shifts)):
-        for row in range(2 * wide + inner):
-            line[which, row, 0:TILE, :] = blank
-            line[which, row, TILE + shots :, :] = blank
-    for load in loads:
-        load.wait()
-
     half = window_ref[0]
-    values = traces_ref[0]
     later = lax.broadcasted_iota(jnp.int32, (length, length), 0)
     earlier = lax.broadcasted_iota(jnp.int32, (length, length), 1)
     near = (jnp.abs(later - earlier) <= half).astype(jnp.float32)
+    sample = lax.broadcasted_iota(jnp.int32, (1, length), 1)
+    count = jnp.minimum(sample + half, length - 1) - jnp.maximum(sample - half, 0) + 1
+    pad[0:HALF_RECV, :] = jnp.zeros((HALF_RECV, length), jnp.float32)
+    tail = pad.shape[0] - HALF_RECV - recv
+    pad[HALF_RECV + recv :, :] = jnp.zeros((tail, length), jnp.float32)
+    load.wait()
+    values = traces_ref[0]
     power = jnp.dot(
         values * values, near,
         precision=lax.Precision.HIGHEST, preferred_element_type=jnp.float32,
     )
-    sample = lax.broadcasted_iota(jnp.int32, (1, length), 1)
-    count = jnp.minimum(sample + half, length - 1) - jnp.maximum(sample - half, 0) + 1
     balanced = values * lax.rsqrt(jnp.maximum(power / count.astype(jnp.float32), FLOOR))
-    pad[0:HALF_RECV, :] = jnp.zeros((HALF_RECV, length), jnp.float32)
     pad[HALF_RECV : HALF_RECV + recv, :] = balanced
-    tail = pad.shape[0] - HALF_RECV - recv
-    pad[HALF_RECV + recv :, :] = jnp.zeros((tail, length), jnp.float32)
 
     def pack(d):
         send[d] = pad[pl.ds(d * inner, rp), :]
@@ -118,6 +104,13 @@
         )
 
     each(1, n, lambda d: outgoing(d).start())
+    blank = jnp.zeros((TILE, length), jnp.float32)
+    for which in range(len(shifts)):
+        for row in range(2 * wide + inner):
+            line[which, row, 0:TILE, :] = blank
+            line[which, row, TILE + shots :, :] = blank
+
+    load_dips.wait()
     for dip in range(-MAXDIP, MAXDIP + 1):
         found = dips_ref[0] == dip
         for i in range(1, dips_ref.shape[0]):
@@ -236,15 +229,14 @@
         out_shape=jax.ShapeDtypeStruct((inner, shots, length), jnp.float32),
         in_specs=[
             pl.BlockSpec(memory_space=pltpu.HBM),
-            pl.BlockSpec(memory_space=pltpu.HBM),
+            pl.BlockSpec(memory_space=pltpu.SMEM),
             pl.BlockSpec(memory_space=pltpu.HBM),
         ],
         out_specs=pl.BlockSpec(memory_space=pltpu.VMEM),
         scratch_shapes=[
             pltpu.VMEM(traces.shape, jnp.float32),
-            pltpu.SMEM(half_window.shape, jnp.int32),
             pltpu.SMEM(dip_slopes.shape, jnp.int32),
-            pltpu.SemaphoreType.DMA((3,)),
+            pltpu.SemaphoreType.DMA((2,)),
             pltpu.VMEM((recv + rp, length), jnp.float32),
             pltpu.VMEM((n, rp, length), jnp.float32),
             pltpu.VMEM(((shots + 4) * rp, length), jnp.float32),

time: 10.8 us -> 10.6 us (0.981)
  Pallas kernels: 9.35 us -> 9.14 us
    pallas_call x1, Pallas kernels: 9.35 us -> 9.14 us  [body(): pl.pallas_call(functools.partial(kernel, n, shots, recv, inner, rp), out_...]
where the time goes in v3:
time: 10.6 us; the launch traced here: 10.4 us
  Pallas kernels  9.14 us (86%)
  between operations  0.66 us (6%)
  local copies, waits for them, and re-layouts  0.6 us (6%)
    pallas_call x1, Pallas kernels, body(): pl.pallas_call(functools.partial(kernel, n, shots, recv, inner, rp), out_...  9.14 us
    transpose x1, local copies, waits for them, and re-layouts, body(): return jnp.swapaxes(result, 0, 1)  0.6 us

profile of v3, /device:TPU:0, one launch (start us, length us, event | category | flops | bytes accessed | tf_op | source)
XLA Modules:
  0.0 10.4 jit_solution(4730052886141311927)
XLA Ops:
  0.7 9.1 %shard_map.37 = f32[2,8,128]{2,1,0:T(8,128)S(1)} custom-call(f32[1,16,128]{2,1,0:T(8,128)} %traces_hbm.1, s32[1]{0:T(128)S(6)} %copy.5.window_ref, s32[9]{0:T(128)} %dips_hbm.1), custom_call_target="tpu_custom_call" | custom-call | tf_op jit(solution)/shard_map/pallas_call | solution.py:227
  9.8 0.6 %copy.4 = f32[8,2,128]{2,1,0:T(2,128)} copy(f32[8,2,128]{2,0,1:T(8,128)S(1)} %bitcast.1) | data formatting | bytes 16384 | tf_op jit(solution)/shard_map/transpose | solution.py:254
